TPU v7x, 32 devices: a whole 2x2x4 slice. The times are simulated.
32 devices in a mesh: dp: 8 (over z, y), fsdp: 2 (over x), section: 2 (over core).
Axes of the slice: x: 2, y: 2, z: 4, core: 2. Of those that a mesh axis runs over, the one named last changes fastest.
Arguments:
- acts: bfloat16 [8192, 5120], P(('dp', 'section'), 'fsdp'), may hold values from -100 to 100
- output_gradient: bfloat16 [8192, 1024], P(('dp', 'section'), 'fsdp'), may hold values from -40 to 40
- lengths: int32 [32], P(('dp', 'section')), may hold values from 1 to 256
- buckets: int32 [32], P(('dp', 'section')), may hold values from 0 to 3
- frozen_key_weight: bfloat16 [5120, 1024], P('fsdp'), may hold values from -0.078125 to 0.078125
- adapter_down_weight: float32 [5120, 128], P('fsdp'), may hold values from -0.078125 to 0.078125
- adapter_up_weight: float32 [128, 1024], P(None, 'fsdp'), may hold values from -0.5 to 0.5
- prompts: bfloat16 [8192, 5120], P(('dp', 'section'), 'fsdp'), may hold values from -6 to 6
Outputs:
- input_gradient: bfloat16 [8192, 5120], P(('dp', 'section'), 'fsdp')
- next_down_weight: float32 [5120, 128], P('fsdp')
- next_up_weight: float32 [128, 1024], P(None, 'fsdp')
- keys: bfloat16 [8192, 1024], P(('dp', 'section'), 'fsdp')
All inputs are finite; a program needn't handle non-finite values.
Results may differ from a plain program's by a relative error of at most 0.0059.
Values may be sent and summed in bfloat16 or wider, within the bound.
A program may use at most 128 MiB of HBM per device.

v0:
```python
import jax
import jax.numpy as jnp
from jax import lax
from jax.sharding import PartitionSpec as P

adapter_scale = 0.5
step_rate = 16.0
clip_norm = 1.0


def per_device(
    acts,
    output_gradient,
    lengths,
    buckets,
    frozen_key_weight,
    adapter_down_weight,
    adapter_up_weight,
    prompts,
):
    tok_rows = acts.shape[0]
    seq_count = lengths.shape[0]
    slot_len = tok_rows // seq_count
    alive_mask = jnp.arange(slot_len, dtype=jnp.int32)[None, :] < lengths[:, None]
    advantage = buckets.astype(jnp.float32)[:, None] - 1.5
    token_weight = jnp.where(alive_mask, advantage, jnp.float32(0.0)).reshape(tok_rows)
    key_gradient = (token_weight[:, None] * output_gradient.astype(jnp.float32)).astype(
        jnp.bfloat16
    )
    first_factor_half = adapter_down_weight.astype(jnp.bfloat16)
    second_factor_half = adapter_up_weight.astype(jnp.bfloat16)
    down_part = jnp.dot(acts, first_factor_half, preferred_element_type=jnp.float32)
    up_part = jnp.dot(key_gradient, second_factor_half.T, preferred_element_type=jnp.float32)
    down_acts, up_grads = lax.psum((down_part, up_part), "fsdp")
    down_weight_half = down_acts.astype(jnp.bfloat16)
    up_weight_half = up_grads.astype(jnp.bfloat16)
    up_gradient = adapter_scale * jnp.dot(
        down_weight_half.T, key_gradient, preferred_element_type=jnp.float32
    )
    down_gradient = adapter_scale * jnp.dot(
        acts.T, up_weight_half, preferred_element_type=jnp.float32
    )
    down_gradient, up_gradient = lax.psum((down_gradient, up_gradient), ("dp", "section"))
    squares = jnp.sum(down_gradient * down_gradient) + jnp.sum(up_gradient * up_gradient)
    squares = lax.psum(squares, "fsdp")
    scale_factor = step_rate * jnp.minimum(1.0, clip_norm / jnp.sqrt(squares + 1e-12))
    next_down_weight = adapter_down_weight - scale_factor * down_gradient
    next_up_weight = adapter_up_weight - scale_factor * up_gradient
    local_product = adapter_scale * jnp.dot(
        up_weight_half, first_factor_half.T, preferred_element_type=jnp.float32
    )
    input_gradient = local_product + jnp.dot(
        lax.all_gather(key_gradient, "fsdp", axis=1, tiled=True),
        frozen_key_weight.T,
        preferred_element_type=jnp.float32,
    )
    weight_column_count = lax.all_to_all(
        frozen_key_weight, "fsdp", split_axis=1, concat_axis=0, tiled=True
    )
    down_whole = lax.all_gather(next_down_weight, "fsdp", axis=0, tiled=True)
    weight_change = jnp.dot(down_whole, next_up_weight, precision=lax.Precision.HIGHEST)
    combined_weight = (
        weight_column_count.astype(jnp.float32) + adapter_scale * weight_change
    ).astype(jnp.bfloat16)
    keys = jnp.dot(
        lax.all_gather(prompts, "fsdp", axis=1, tiled=True),
        combined_weight,
        preferred_element_type=jnp.float32,
    )
    return (
        input_gradient.astype(jnp.bfloat16),
        next_down_weight,
        next_up_weight,
        keys.astype(jnp.bfloat16),
    )


def solution(mesh):
    placed = (
        P(("dp", "section"), "fsdp"),
        P(("dp", "section"), "fsdp"),
        P(("dp", "section")),
        P(("dp", "section")),
        P("fsdp", None),
        P("fsdp", None),
        P(None, "fsdp"),
        P(("dp", "section"), "fsdp"),
    )
    return jax.shard_map(
        per_device,
        mesh=mesh,
        in_specs=placed,
        out_specs=(
            P(("dp", "section"), "fsdp"),
            P("fsdp", None),
            P(None, "fsdp"),
            P(("dp", "section"), "fsdp"),
        ),
        check_vma=False,
    )
```

profile of v0, /device:TPU:0, one launch (start us, length us, event | category | flops | bytes accessed | tf_op | source)
XLA Modules:
  0.0 316.1 jit_solution(12598753931631406176)
XLA Ops:
  9.6 1.2 multiply_convert_fusion
  10.8 2.1 fusion.7
  13.0 2.2 fusion.3
  15.1 20.0 %all-reduce.6 = (bf16[512,128]{1,0:T(8,128)(2,1)S(1)}, bf16[512,128]{1,0:T(8,128)(2,1)}) all-reduce(f32[512,128]{1,0:T(8,128)} %fusion.7, f32[512,128]{1,0:T(8,128)S(1)} %fusion.3), channel_id=1, replica_groups=mesh['dp'=8,'fsdp'=2,'section'=2] {'fsdp'}, use_global_device_ids=true, to_apply=%region_0.1 | all-reduce | flops 131072 | bytes 786432 | tf_op jit(solution)/shard_map/psum | solution.py:34
  35.1 1.9 convolution_multiply_fusion.1
  36.9 1.6 fusion.1
  39.2 95.5 %all-reduce.5.cloned.1.call-done = (f32[2560,128]{0,1:T(8,128)}, f32[128,512]{1,0:T(8,128)}) async-done(((f32[2560,128]{0,1:T(8,128)}, f32[128,512]{1,0:T(8,128)}), (f32[2560,128]{0,1:T(8,128)}, f32[128,512]{1,0:T(8,128)})) %all-reduce.5.cloned.1.call-update) | async-done | bytes 1572880 | tf_op jit(solution)/shard_map/psum | solution.py:43
  134.7 1.7 multiply_reduce_fusion.1
  136.4 2.3 multiply_reduce_fusion
  140.0 1.5 copy.18
  141.4 5.4 %psum.39 = f32[]{:T(128)} all-reduce(f32[]{:T(128)S(6)} %add.25), channel_id=1, replica_groups=mesh['dp'=8,'fsdp'=2,'section'=2] {'fsdp'}, use_global_device_ids=true, to_apply=%region_6.7 | all-reduce | flops 1 | bytes 8 | tf_op jit(solution)/shard_map/psum | solution.py:45
  147.6 2.6 multiply_subtract_fusion
  150.7 8.1 %copy.19 = bf16[2560,1024]{0,1:T(8,128)(2,1)} copy(bf16[2560,1024]{1,0:T(8,128)(2,1)} %param.12) | data formatting | bytes 10485760 | tf_op args[4]
  158.8 6.3 %all-to-all-start = ((bf16[2560,2,512]{0,2,1:T(8,128)(2,1)}), bf16[2560,2,512]{0,2,1:T(8,128)(2,1)}, u32[]{:S(2)}, u32[]{:S(2)}) async-start(bf16[2560,2,512]{0,2,1:T(8,128)(2,1)} %bitcast.27), calls=%async_computation | async-start | bytes 10485760 | tf_op jit(solution)/shard_map/all_to_all | solution.py:57
  165.1 1.5 copy.21
  166.7 5.2 %fusion.12 = f32[512,2560]{1,0:T(8,128)S(1)} fusion(bf16[512,1024]{1,0:T(8,128)(2,1)} %all-gather.4.cloned.1.call-done, bf16[2560,1024]{1,0:T(8,128)(2,1)} %param.12), kind=kOutput, calls=%fused_computation.25 | convolution fusion | flops 2684354560 | bytes 11534336 | tf_op jit(solution)/shard_map/dot_general | solution.py:52
  171.9 2.4 add_convert_fusion
  174.3 89.6 %all-to-all-done = bf16[2560,2,512]{0,2,1:T(8,128)(2,1)} async-done(((bf16[2560,2,512]{0,2,1:T(8,128)(2,1)}), bf16[2560,2,512]{0,2,1:T(8,128)(2,1)}, u32[]{:S(2)}, u32[]{:S(2)}) %all-to-all-start) | async-done | bytes 5242912 | tf_op jit(solution)/shard_map/all_to_all | solution.py:57
  263.9 7.8 %convert_bitcast_fusion = f32[2,2560,512]{1,2,0:T(8,128)} fusion(bf16[2560,2,512]{0,2,1:T(8,128)(2,1)} %all-to-all-done), kind=kLoop, calls=%fused_computation.2 | loop fusion | flops 2621440 | bytes 15728640 | tf_op jit(solution)/shard_map/convert_element_type | solution.py:63
  271.6 11.4 %copy.20 = f32[2,2560,512]{2,1,0:T(8,128)} copy(f32[2,2560,512]{1,2,0:T(8,128)} %convert_bitcast_fusion) | data formatting | bytes 20971520 | tf_op jit(solution)/shard_map/convert_element_type | solution.py:63
  283.0 13.4 %fusion = bf16[5120,512]{1,0:T(8,128)(2,1)} fusion(f32[2,2560,512]{2,1,0:T(8,128)} %copy.20, f32[5120,128]{0,1:T(8,128)} %all-gather.6.cloned.1.call-done, f32[128,512]{1,0:T(8,128)S(1)} %multiply_subtract_fusion.1), kind=kOutput, calls=%fused_computation.1 | convolution fusion | flops 4034396160 | bytes 18612224 | tf_op jit(solution)/shard_map/dot_general | solution.py:61
  296.5 3.9 %all-gather.8.cloned.1.call-done = bf16[512,5120]{1,0:T(8,128)(2,1)} async-done(((bf16[512,2560]{1,0:T(8,128)(2,1)}), bf16[512,5120]{1,0:T(8,128)(2,1)}) %all-gather.8.cloned.1.call-update) | async-done | bytes 5242896 | tf_op jit(solution)/shard_map/all_gather | solution.py:66
  300.4 7.1 %fusion.2 = bf16[512,512]{0,1:T(8,128)(2,1)S(1)} fusion(bf16[5120,512]{1,0:T(8,128)(2,1)} %fusion, bf16[512,5120]{1,0:T(8,128)(2,1)} %all-gather.8.cloned.1.call-done), kind=kOutput, calls=%fused_computation.9 | convolution fusion | flops 2684616704 | bytes 11010048 | tf_op jit(solution)/shard_map/dot_general | solution.py:65
  307.5 1.0 copy.22
  (32 shorter events, 2.9 us)
Async XLA Ops:
  8.0 5.0 %copy-start = (bf16[512,2560]{1,0:T(8,128)(2,1)S(1)}, bf16[512,2560]{1,0:T(8,128)(2,1)}, u32[]{:S(2)}) copy-start(bf16[512,2560]{1,0:T(8,128)(2,1)} %param.8) | copy-start | bytes 7864324
  8.0 126.7 %all-reduce.5.cloned.1.call-start = ((), (), s32[]{:S(2)}) async-start(), calls=%async_computation.4 | async-start | bytes 3145728 | tf_op jit(solution)/shard_map/psum | solution.py:43
  10.8 24.3 %copy-start.4 = (bf16[512,512]{1,0:T(8,128)(2,1)}, bf16[512,512]{1,0:T(8,128)(2,1)S(1)}, u32[]{:S(2)}) copy-start(bf16[512,512]{1,0:T(8,128)(2,1)S(1)} %multiply_convert_fusion) | copy-start | bytes 1572868
  38.5 101.4 %copy-start.2 = (f32[2560,128]{1,0:T(8,128)S(1)}, f32[2560,128]{1,0:T(8,128)}, u32[]{:S(2)}) copy-start(f32[2560,128]{1,0:T(8,128)} %param.13) | copy-start | bytes 3932164
  38.6 128.1 %all-gather.4.cloned.1.call-start = ((), (), s32[]{:S(2)}) async-start(), calls=%async_computation.1 | async-start | bytes 1572864 | tf_op jit(solution)/shard_map/all_gather | solution.py:53
  39.1 243.9 %all-gather.6.cloned.1.call-start = ((), (), s32[]{:S(2)}) async-start(), calls=%async_computation.2 | async-start | bytes 3932160 | tf_op jit(solution)/shard_map/all_gather | solution.py:60
  134.7 12.9 %copy-start.5 = (f32[2560,128]{0,1:T(8,128)S(1)}, f32[2560,128]{0,1:T(8,128)}, u32[]{:S(2)}) copy-start(f32[2560,128]{0,1:T(8,128)} %get-tuple-element.16) | copy-start | bytes 3932164
  150.2 150.3 %all-gather.8.cloned.1.call-start = ((), (), s32[]{:S(2)}) async-start(), calls=%async_computation.3 | async-start | bytes 7864320 | tf_op jit(solution)/shard_map/all_gather | solution.py:66
  158.8 6.3 %copy-start.3 = (f32[2560,128]{0,1:T(8,128)S(1)}, f32[2560,128]{0,1:T(8,128)}, u32[]{:S(2)}) copy-start(f32[2560,128]{0,1:T(8,128)} %multiply_subtract_fusion) | copy-start | bytes 3932164
  158.8 105.1 %all-to-all-start = ((bf16[2560,2,512]{0,2,1:T(8,128)(2,1)}), bf16[2560,2,512]{0,2,1:T(8,128)(2,1)}, u32[]{:S(2)}, u32[]{:S(2)}) async-start(bf16[2560,2,512]{0,2,1:T(8,128)(2,1)} %bitcast.27), calls=%async_computation | async-start | bytes 10485760 | tf_op jit(solution)/shard_map/all_to_all | solution.py:57
  165.1 1.5 copy-start.7
  165.1 1.5 copy-start.8
  166.6 116.4 %copy-start.6 = (f32[128,512]{1,0:T(8,128)}, f32[128,512]{1,0:T(8,128)S(1)}, u32[]{:S(2)}) copy-start(f32[128,512]{1,0:T(8,128)S(1)} %multiply_subtract_fusion.1) | copy-start | bytes 786436
  300.4 8.1 %copy-start.1 = (bf16[512,2560]{1,0:T(8,128)(2,1)S(1)}, bf16[512,2560]{1,0:T(8,128)(2,1)}, u32[]{:S(2)}) copy-start(bf16[512,2560]{1,0:T(8,128)(2,1)} %param.8) | copy-start | bytes 7864324
Sparse Core Ops, SparseCore 0:
  38.7 95.9 all-reduce.4
Sparse Core Ops, SparseCore 1:
  41.2 21.5 all-gather.3
  150.2 59.4 all-gather.5
  211.1 89.2 all-gather.7
where the time goes:
time: 317 us; the launch traced here: 316 us
  waiting for transfers between devices  190 us (60%)
  matrix products  35.9 us (11%)
  blocking collectives  25.4 us (8%)
  local copies, waits for them, and re-layouts  23.5 us (7%)
  between operations  17.8 us (6%)
  other arithmetic  17.1 us (5%)
  starting transfers between devices  6.44 us (2%)
    psum x1, waiting for transfers between devices, per_device(): lax.psum((down_gradient, up_gradient), ('dp', 'section'))  95.5 us
    all_to_all x1, waiting for transfers between devices, per_device(): lax.all_to_all(frozen_key_weight, 'fsdp', split_axis=1, concat_axis=0, ti...  89.6 us
    psum x1, blocking collectives, per_device(): down_acts, up_grads = lax.psum((down_part, up_part), 'fsdp')  20 us
    dot_general x1, matrix products, per_device(): jnp.dot(down_whole, next_up_weight, precision=lax.Precision.HIGHEST)  13.4 us
    unnamed x23, local copies, waits for them, and re-layouts  12.1 us
    convert_element_type x1, local copies, waits for them, and re-layouts, per_device(): weight_column_count.astype(jnp.float32) + adapter_scale * weight_change  11.4 us
    convert_element_type x1, other arithmetic, per_device(): weight_column_count.astype(jnp.float32) + adapter_scale * weight_change  7.77 us
    dot_general x1, matrix products, per_device(): jnp.dot(lax.all_gather(prompts, 'fsdp', axis=1, tiled=True), combined_wei...  7.1 us
  transfers between devices with their start and end apart: 5, of which 3 were waited for; matrix products, arithmetic and copies ran while one was open for 18% of the time, Pallas kernels for 0%

commit v1 on v0

v1 whole, which is shorter than its diff:
```python
import functools

import jax
import jax.numpy as jnp
from jax import lax
from jax.experimental import pallas as pl
from jax.experimental.pallas import tpu as pltpu
from jax.sharding import PartitionSpec as P

ADAPTER_SCALE = 0.5
STEP_RATE = 16.0
CLIP_NORM = 1.0
MESH = pl.DeviceIdType.MESH
F32 = jnp.float32
BF16 = jnp.bfloat16
NT = (((1,), (1,)), ((), ()))


class Plan:
    def __init__(self, mesh, rows, width, channels, rank):
        self.fsdp = mesh.shape["fsdp"]
        self.cores = mesh.shape["section"]
        dp = mesh.shape["dp"]
        self.outer = 4 if dp % 4 == 0 else 1
        self.inner = dp // self.outer
        self.rows, self.width, self.channels, self.rank = rows, width, channels, rank
        span = self.cores * self.inner
        self.unit = 256 if width % 256 == 0 and channels % 256 == 0 else 128
        units = (width + channels) // self.unit
        self.chunks = -(-units // span)
        self.down_units = width // self.unit
        self.units = units
        self.tile = 256 if width % 256 == 0 else 128


def kernel(
    plan,
    lengths, buckets, acts_h, og_h, frozen_h, down_h, up_h, prompts_h,
    ig_h, nd_h, nu_h, keys_h,
    acts, og, frozen, down, up, prompts,
    a_half, gk, proj_send, proj_recv, pd, pg,
    kp_own, kp_send, kp_recv,
    gbuf, core_recv, y_send, y_recv, quarter, z_send, z_recv, ag, sq,
    ig, nd, nu, keys,
    load_sem, store_sem, x_send_sem, x_recv_sem, d_send_sem, d_recv_sem, q_send_sem, q_recv_sem,
):
    F, S, I, O, K = plan.fsdp, plan.cores, plan.inner, plan.outer, plan.chunks
    U, W, C = plan.unit, plan.width, plan.channels
    T = plan.rows
    x = lax.axis_index("fsdp")
    dp = lax.axis_index("dp")
    core = lax.axis_index("section")
    zi, yi = dp // I, dp % I

    loads = {}
    for n, (name, src, dst) in enumerate((
        ("og", og_h, og), ("up", up_h, up), ("acts", acts_h, acts), ("down", down_h, down),
        ("prompts", prompts_h, prompts), ("frozen", frozen_h, frozen),
    )):
        loads[name] = pltpu.make_async_copy(src, dst, load_sem.at[n])
        loads[name].start()

    x_peer = [lax.rem(x + d, F) for d in range(F)]
    x_from = [lax.rem(x + F - d, F) for d in range(F)]
    y_peer = [lax.rem(yi + d, I) for d in range(I)]
    y_from = [lax.rem(yi + I - d, I) for d in range(I)]
    z_peer = [lax.rem(zi + d, O) for d in range(O)]
    z_from = [lax.rem(zi + O - d, O) for d in range(O)]

    def x_id(d):
        return {"fsdp": x_peer[d]}

    def y_id(d):
        return {"dp": zi * I + y_peer[d]}

    def z_id(d):
        return {"dp": z_peer[d] * I + yi}

    core_id = {"section": 1 - core}
    others = (
        [x_id(d) for d in range(1, F)] + [y_id(d) for d in range(1, I)]
        + [z_id(d) for d in range(1, O)] + [core_id]
    )
    barrier = pltpu.get_barrier_semaphore()
    for other in others:
        pl.semaphore_signal(barrier, inc=1, device_id=other, device_id_type=MESH)

    sent = []

    def send(src, dst, ssem, rsem, to):
        copy = pltpu.make_async_remote_copy(
            src_ref=src, dst_ref=dst, send_sem=ssem, recv_sem=rsem, device_id=to, device_id_type=MESH
        )
        copy.start()
        sent.append(copy)

    def arrive(src, dst, ssem, rsem, to):
        pltpu.make_async_remote_copy(
            src_ref=src, dst_ref=dst, send_sem=ssem, recv_sem=rsem, device_id=to, device_id_type=MESH
        ).wait_recv()

    def proj_exchange(n, value):
        proj_send[n] = value.astype(BF16)
        for d in range(1, F):
            send(proj_send.at[n], proj_recv.at[n, d], x_send_sem.at[n, d], x_recv_sem.at[n, d], x_id(d))

    def proj_sum(n, value):
        for d in range(1, F):
            arrive(proj_send.at[n], proj_recv.at[n, d], x_send_sem.at[n, d], x_recv_sem.at[n, d], x_id(d))
            value = value + proj_recv[n, d].astype(F32)
        return value

    loads["og"].wait()
    loads["up"].wait()
    slot = T // lengths.shape[0]
    position = lax.broadcasted_iota(jnp.int32, (slot, C), 0)
    for i in range(lengths.shape[0]):
        weight = jnp.where(position < lengths[i], buckets[i].astype(F32) - 1.5, 0.0)
        block = og[i * slot:(i + 1) * slot, :].astype(F32)
        gk[x, i * slot:(i + 1) * slot, :] = (weight * block).astype(BF16)
    mine = gk[x]
    up_part = lax.dot_general(mine, up[...].astype(BF16), NT, preferred_element_type=F32)
    pl.semaphore_wait(barrier, len(others))
    proj_exchange(0, up_part)

    loads["acts"].wait()
    loads["down"].wait()
    a_half[...] = down[...].astype(BF16)
    down_part = jnp.dot(acts[...], a_half[...], preferred_element_type=F32)
    proj_exchange(1, down_part)

    loads["prompts"].wait()
    loads["frozen"].wait()
    tile_c = min(256, C)

    def frozen_part(owner, put):
        @pl.loop(0, C // tile_c)
        def _(t):
            cols = pl.ds(pl.multiple_of(t * tile_c, tile_c), tile_c)
            src = pl.ds(pl.multiple_of(owner * C + t * tile_c, tile_c), tile_c)
            put(cols, jnp.dot(prompts[...], frozen[:, src], preferred_element_type=F32))

    for d in range(1, F):
        def put_other(cols, value, d=d):
            kp_send[d, :, cols] = value.astype(BF16)

        frozen_part(x_peer[d], put_other)

    up_half = proj_sum(0, up_part)
    up_half_t = up_half.T.astype(BF16)
    up_half = up_half.astype(BF16)
    down_half_t = None

    def core_copy(k):
        return (gbuf.at[k, 1 - core], core_recv.at[k], d_send_sem.at[k, 0], d_recv_sem.at[k, 0], core_id)

    for k in range(K):
        for s in range(S):
            for i in range(I):
                n = (k * S + s) * I + i
                if n < plan.down_units:
                    part = jnp.dot(up_half_t, acts[:, n * U:(n + 1) * U], preferred_element_type=F32)
                elif n < plan.units:
                    if down_half_t is None:
                        down_half_t = proj_sum(1, down_part).T.astype(BF16)
                    m = n - plan.down_units
                    part = jnp.dot(down_half_t, gk[x, :, m * U:(m + 1) * U], preferred_element_type=F32)
                else:
                    part = jnp.zeros((plan.rank, U), F32)
                gbuf[k, s, i] = ADAPTER_SCALE * part
        send(*core_copy(k))

    for d in range(1, F):
        send(gk.at[x], gk.at[x], x_send_sem.at[2, d], x_recv_sem.at[2, d], x_id(d))
    for d in range(1, F):
        send(kp_send.at[d], kp_recv.at[d], x_send_sem.at[3, d], x_recv_sem.at[3, d], x_id(d))

    def y_copy(k, d):
        return (y_send.at[k, d], y_recv.at[k, d], d_send_sem.at[k, d], d_recv_sem.at[k, d], y_id(d))

    def z_copy(k, d):
        e = I + d
        return (z_send.at[k, z_peer[d]], z_recv.at[k, d], d_send_sem.at[k, e], d_recv_sem.at[k, e], z_id(d))

    for k in range(K):
        arrive(*core_copy(k))
        for d in range(I):
            value = gbuf[k, core, y_peer[d]] + core_recv[k, y_peer[d]]
            if d == 0:
                quarter[k] = value
            else:
                y_send[k, d] = value.astype(BF16)
                send(*y_copy(k, d))

    def put_own(cols, value):
        kp_own[:, cols] = value

    frozen_part(x, put_own)
    pd[...] = jnp.dot(prompts[...], a_half[...], preferred_element_type=F32)

    part_rows = plan.rank // O
    for k in range(K):
        value = quarter[k]
        for d in range(1, I):
            arrive(*y_copy(k, d))
            value = value + y_recv[k, d].astype(F32)
        quarter[k] = value
        for o in range(O):
            z_send[k, o] = value[o * part_rows:(o + 1) * part_rows].astype(BF16)
        for d in range(1, O):
            send(*z_copy(k, d))

    base = I + O

    def ag_z(k, d, slot):
        e = base + d
        return (ag.at[k, core, yi, zi], ag.at[k, core, yi, slot], d_send_sem.at[k, e], d_recv_sem.at[k, e], z_id(d))

    def ag_y(k, d, slot):
        e = base + O + d
        return (ag.at[k, core, yi], ag.at[k, core, slot], d_send_sem.at[k, e], d_recv_sem.at[k, e], y_id(d))

    def ag_core(k, slot):
        e = base + O + I
        return (ag.at[k, core], ag.at[k, slot], d_send_sem.at[k, e], d_recv_sem.at[k, e], core_id)

    squares = jnp.zeros((part_rows, U), F32)
    for k in range(K):
        value = quarter[k, pl.ds(pl.multiple_of(zi * part_rows, part_rows), part_rows), :]
        for d in range(1, O):
            arrive(*z_copy(k, d))
            value = value + z_recv[k, d].astype(F32)
        rounded = value.astype(BF16)
        ag[k, core, yi, zi] = rounded
        for d in range(1, O):
            send(*ag_z(k, d, zi))
        value = rounded.astype(F32)
        squares = squares + value * value

    def sq_send(stage, value, own, count, to):
        sq[stage, own] = value
        for d in range(1, count):
            send(sq.at[stage, own], sq.at[stage, own], q_send_sem.at[stage, d], q_recv_sem.at[stage, d], to(d))

    def sq_sum(stage, own, count, to, source):
        for d in range(1, count):
            arrive(sq.at[stage, own], sq.at[stage, source(d)], q_send_sem.at[stage, d], q_recv_sem.at[stage, d], to(d))
        total = sq[stage, 0]
        for n in range(1, count):
            total = total + sq[stage, n]
        return total

    total = jnp.broadcast_to(jnp.sum(squares, keepdims=True), (8, 128))
    sq_send(0, total, zi, O, z_id)

    for k in range(K):
        for d in range(1, O):
            arrive(*ag_z(k, d, z_from[d]))
        for d in range(1, I):
            send(*ag_y(k, d, yi))
    total = sq_sum(0, zi, O, z_id, lambda d: z_from[d])
    sq_send(1, total, yi, I, y_id)

    for d in range(1, F):
        arrive(gk.at[x], gk.at[x_from[d]], x_send_sem.at[2, d], x_recv_sem.at[2, d], x_id(d))
    tile = plan.tile

    def ig_tile(t):
        span = pl.ds(pl.multiple_of(t * tile, tile), tile)
        value = ADAPTER_SCALE * lax.dot_general(up_half, a_half[span, :], NT, preferred_element_type=F32)
        for p in range(F):
            value = value + lax.dot_general(
                gk[p], frozen[span, p * C:(p + 1) * C], NT, preferred_element_type=F32
            )
        ig[:, span] = value.astype(BF16)

    pl.loop(0, W // tile)(ig_tile)
    ig_store = pltpu.make_async_copy(ig, ig_h, store_sem.at[0])
    ig_store.start()

    for k in range(K):
        for d in range(1, I):
            arrive(*ag_y(k, d, y_from[d]))
        send(*ag_core(k, core))
    total = sq_sum(1, yi, I, y_id, lambda d: y_from[d])
    sq_send(2, total, core, S, lambda d: core_id)
    total = sq_sum(2, core, S, lambda d: core_id, lambda d: 1 - core)
    sq_send(3, total, x, F, x_id)

    def unit_of(n):
        k, s, i = n // (S * I), (n // I) % S, n % I
        return ag[k, s, i].reshape(plan.rank, U)

    low = jnp.zeros((T, plan.rank), F32)
    for k in range(K):
        arrive(*ag_core(k, 1 - core))
        for n in range(k * S * I, (k + 1) * S * I):
            if n < plan.down_units:
                low = low + lax.dot_general(
                    prompts[:, n * U:(n + 1) * U], unit_of(n), NT, preferred_element_type=F32
                )
    total = sq_sum(3, x, F, x_id, lambda d: x_from[d])
    norm = jnp.sqrt(total + 1e-12)
    factor = (STEP_RATE * jnp.minimum(1.0, CLIP_NORM / norm))[0:1, 0:1]

    pg[...] = pd[...] - factor * low
    proj_exchange(2, pg[...])

    for n in range(plan.units):
        if n < plan.down_units:
            span = slice(n * U, (n + 1) * U)
            nd[span, :] = down[span, :] - factor * unit_of(n).astype(F32).T
        else:
            span = slice((n - plan.down_units) * U, (n - plan.down_units + 1) * U)
            nu[:, span] = up[:, span] - factor * unit_of(n).astype(F32)
    nd_store = pltpu.make_async_copy(nd, nd_h, store_sem.at[1])
    nd_store.start()
    nu_store = pltpu.make_async_copy(nu, nu_h, store_sem.at[2])
    nu_store.start()

    for d in range(1, F):
        arrive(kp_send.at[d], kp_recv.at[d], x_send_sem.at[3, d], x_recv_sem.at[3, d], x_id(d))
        kp_own[...] = kp_own[...] + kp_recv[d].astype(F32)
    low_half = (ADAPTER_SCALE * proj_sum(2, pg[...])).astype(BF16)
    keys[...] = (
        kp_own[...] + jnp.dot(low_half, nu[...].astype(BF16), preferred_element_type=F32)
    ).astype(BF16)
    keys_store = pltpu.make_async_copy(keys, keys_h, store_sem.at[3])
    keys_store.start()

    for copy in sent:
        copy.wait_send()
    ig_store.wait()
    nd_store.wait()
    nu_store.wait()
    keys_store.wait()


def per_device(mesh, acts, output_gradient, lengths, buckets, frozen, down, up, prompts):
    T, W = acts.shape
    C = output_gradient.shape[1]
    R = down.shape[1]
    plan = Plan(mesh, T, W, C, R)
    F, S, I, O, K, U = plan.fsdp, plan.cores, plan.inner, plan.outer, plan.chunks, plan.unit
    N = C * F
    smem = pl.BlockSpec(memory_space=pltpu.SMEM)
    hbm = pl.BlockSpec(memory_space=pl.ANY)
    dma = pltpu.SemaphoreType.DMA
    hops = I + O + O + I + 1
    scratch = [
        pltpu.VMEM((T, W), BF16), pltpu.VMEM((T, C), BF16), pltpu.VMEM((W, N), BF16),
        pltpu.VMEM((W, R), F32), pltpu.VMEM((R, C), F32), pltpu.VMEM((T, W), BF16),
        pltpu.VMEM((W, R), BF16), pltpu.VMEM((F, T, C), BF16),
        pltpu.VMEM((3, T, R), BF16), pltpu.VMEM((3, F, T, R), BF16),
        pltpu.VMEM((T, R), F32), pltpu.VMEM((T, R), F32),
        pltpu.VMEM((T, C), F32), pltpu.VMEM((F, T, C), BF16), pltpu.VMEM((F, T, C), BF16),
        pltpu.VMEM((K, S, I, R, U), F32), pltpu.VMEM((K, I, R, U), F32),
        pltpu.VMEM((K, I, R, U), BF16), pltpu.VMEM((K, I, R, U), BF16),
        pltpu.VMEM((K, R, U), F32),
        pltpu.VMEM((K, O, R // O, U), BF16), pltpu.VMEM((K, O, R // O, U), BF16),
        pltpu.VMEM((K, S, I, O, R // O, U), BF16),
        pltpu.VMEM((4, max(O, I, S, F), 8, 128), F32),
        pltpu.VMEM((T, W), BF16), pltpu.VMEM((W, R), F32), pltpu.VMEM((R, C), F32), pltpu.VMEM((T, C), BF16),
        dma((6,)), dma((4,)), dma((4, F)), dma((4, F)), dma((K, hops)), dma((K, hops)),
        dma((4, max(O, I, S, F))), dma((4, max(O, I, S, F))),
    ]
    return pl.pallas_call(
        functools.partial(kernel, plan),
        out_shape=(
            jax.ShapeDtypeStruct((T, W), BF16),
            jax.ShapeDtypeStruct((W, R), F32),
            jax.ShapeDtypeStruct((R, C), F32),
            jax.ShapeDtypeStruct((T, C), BF16),
        ),
        in_specs=[smem, smem] + [hbm] * 6,
        out_specs=(hbm,) * 4,
        scratch_shapes=scratch,
        compiler_params=pltpu.CompilerParams(
            collective_id=0, has_side_effects=True, vmem_limit_bytes=48 * 1024 * 1024
        ),
        cost_estimate=pl.CostEstimate(
            flops=2 * T * W * (2 * N + 4 * R), bytes_accessed=2 * (3 * T * W + W * N), transcendentals=0
        ),
        name="adapter_step",
    )(lengths, buckets, acts, output_gradient, frozen, down, up, prompts)


def solution(mesh):
    tokens = P(("dp", "section"), "fsdp")
    return jax.shard_map(
        functools.partial(per_device, mesh),
        mesh=mesh,
        in_specs=(
            tokens, tokens, P(("dp", "section")), P(("dp", "section")),
            P("fsdp", None), P("fsdp", None), P(None, "fsdp"), tokens,
        ),
        out_specs=(tokens, P("fsdp", None), P(None, "fsdp"), tokens),
        check_vma=False,
    )
```

time: 317 us -> 55.8 us (0.18)
  waiting for transfers between devices: 190 us -> 0 us
  Pallas kernels: 0 us -> 44.3 us
  matrix products: 35.9 us -> 0 us
  blocking collectives: 25.4 us -> 0 us
  between operations: 17.8 us -> 0.66 us
  other arithmetic: 17.1 us -> 0 us
  local copies, waits for them, and re-layouts: 23.5 us -> 10.6 us
  starting transfers between devices: 6.44 us -> 0 us
    psum x1 -> x0, waiting for transfers between devices: 95.5 us -> none  [per_device(): lax.psum((down_gradient, up_gradient), ('dp', 'section'))]
    all_to_all x1 -> x0, waiting for transfers between devices: 89.6 us -> none  [per_device(): lax.all_to_all(frozen_key_weight, 'fsdp', split_axis=1, concat_axis=0, ti...]
    pallas_call x0 -> x1, Pallas kernels: none -> 44.3 us  [per_device(): pl.pallas_call(functools.partial(kernel, plan), out_shape=(jax.ShapeDtype...]
    dot_general x8 -> x0, matrix products: 35.9 us -> none  [the longest x1 13.4 us: per_device(): jnp.dot(down_whole, next_up_weight, precision=lax.Precision.HIGHEST)]
    psum x2 -> x0, blocking collectives: 25.4 us -> none  [the longest x1 20 us: per_device(): down_acts, up_grads = lax.psum((down_part, up_part), 'fsdp')]
    convert_element_type x1 -> x0, local copies, waits for them, and re-layouts: 11.4 us -> none  [per_device(): weight_column_count.astype(jnp.float32) + adapter_scale * weight_change]
    convert_element_type x2 -> x0, other arithmetic: 8.97 us -> none  [the longest x1 7.77 us: per_device(): weight_column_count.astype(jnp.float32) + adapter_scale * weight_change]
    all_to_all x1 -> x0, starting transfers between devices: 6.28 us -> none  [per_device(): lax.all_to_all(frozen_key_weight, 'fsdp', split_axis=1, concat_axis=0, ti...]
  transfers between devices with their start and end apart: 5 -> 0, of which waited for: 3 -> 0; matrix products, arithmetic and copies ran while one was open for 18% -> 0% of each run, Pallas kernels for 0% -> 0%
where the time goes in v1:
time: 55.8 us; the launch traced here: 55.5 us
  Pallas kernels  44.3 us (79%)
  local copies, waits for them, and re-layouts  10.6 us (19%)
  between operations  0.66 us (1%)
    pallas_call x1, Pallas kernels, per_device(): pl.pallas_call(functools.partial(kernel, plan), out_shape=(jax.ShapeDtype...  44.3 us
    unnamed x14, local copies, waits for them, and re-layouts  10.6 us

profile of v1, /device:TPU:0, one launch (start us, length us, event | category | flops | bytes accessed | tf_op | source)
XLA Modules:
  0.0 55.5 jit_solution(7991050664600242389)
XLA Ops:
  0.6 0.0 copy-start
  0.6 1.3 %copy-done = f32[2560,128]{1,0:T(8,128)S(1)} copy-done((f32[2560,128]{1,0:T(8,128)S(1)}, f32[2560,128]{1,0:T(8,128)}, u32[]{:S(2)}) %copy-start) | copy-done | bytes 1310744
  2.0 0.0 copy-start.1
  2.0 1.0 %copy-done.1 = bf16[512,512]{1,0:T(8,128)(2,1)S(1)} copy-done((bf16[512,512]{1,0:T(8,128)(2,1)S(1)}, bf16[512,512]{1,0:T(8,128)(2,1)}, u32[]{:S(2)}) %copy-start.1) | copy-done | bytes 524312
  3.0 0.0 copy-start.2
  3.0 0.9 %copy-done.2 = f32[128,512]{1,0:T(8,128)S(1)} copy-done((f32[128,512]{1,0:T(8,128)S(1)}, f32[128,512]{1,0:T(8,128)}, u32[]{:S(2)}) %copy-start.2) | copy-done | bytes 262168
  3.9 0.0 copy-start.3
  3.9 0.7 %copy-done.3 = s32[2]{0:T(128)S(1)} copy-done((s32[2]{0:T(128)S(1)}, s32[2]{0:T(128)}, u32[]{:S(2)}) %copy-start.3) | copy-done | bytes 32
  4.6 0.0 copy-start.4
  4.6 0.7 %copy-done.4 = s32[2]{0:T(128)S(1)} copy-done((s32[2]{0:T(128)S(1)}, s32[2]{0:T(128)}, u32[]{:S(2)}) %copy-start.4) | copy-done | bytes 32
  5.3 44.3 %adapter_step.1 = (bf16[512,2560]{1,0:T(8,128)(2,1)}, f32[2560,128]{1,0:T(8,128)S(1)}, f32[128,512]{1,0:T(8,128)S(1)}, bf16[512,512]{1,0:T(8,128)(2,1)S(1)}) custom-call(s32[2]{0:T(128)S(1)} %copy-done.3, s32[2]{0:T(128)S(1)} %copy-done.4, bf16[512,2560]{1,0:T(8,128)(2,1)} %acts_h.1, bf16[512,512]{1,0:T(8,128)(2,1)S(1)} %copy-done.1, ...), custom_call_target="tpu_custom_call" | custom-call | flops 6710886400 | bytes 13107200 | tf_op jit(solution)/shard_map/adapter_step/pallas_call | solution.py:367
  49.5 3.4 %copy.16 = bf16[512,2560]{1,0:T(8,128)(2,1)} copy(bf16[512,2560]{1,0:T(8,128)(2,1)} %get-tuple-element.8) | data formatting | bytes 5242880
  52.9 1.1 %copy.17 = f32[2560,128]{1,0:T(8,128)} copy(f32[2560,128]{1,0:T(8,128)S(1)} %get-tuple-element.9) | data formatting | bytes 2621440
  54.0 0.7 %copy.18 = f32[128,512]{1,0:T(8,128)} copy(f32[128,512]{1,0:T(8,128)S(1)} %get-tuple-element.10) | data formatting | bytes 524288
  54.7 0.8 %copy.19 = bf16[512,512]{1,0:T(8,128)(2,1)} copy(bf16[512,512]{1,0:T(8,128)(2,1)S(1)} %get-tuple-element.11) | data formatting | bytes 1048576
Async XLA Ops:
  0.6 1.3 %copy-start = (f32[2560,128]{1,0:T(8,128)S(1)}, f32[2560,128]{1,0:T(8,128)}, u32[]{:S(2)}) copy-start(f32[2560,128]{1,0:T(8,128)} %down_h.1) | copy-start | bytes 3932164
  2.0 1.0 %copy-start.1 = (bf16[512,512]{1,0:T(8,128)(2,1)S(1)}, bf16[512,512]{1,0:T(8,128)(2,1)}, u32[]{:S(2)}) copy-start(bf16[512,512]{1,0:T(8,128)(2,1)} %og_h.1) | copy-start | bytes 1572868
  3.0 0.9 %copy-start.2 = (f32[128,512]{1,0:T(8,128)S(1)}, f32[128,512]{1,0:T(8,128)}, u32[]{:S(2)}) copy-start(f32[128,512]{1,0:T(8,128)} %up_h.1) | copy-start | bytes 786436
  3.9 0.7 %copy-start.3 = (s32[2]{0:T(128)S(1)}, s32[2]{0:T(128)}, u32[]{:S(2)}) copy-start(s32[2]{0:T(128)} %lengths.1) | copy-start | bytes 28
  4.6 0.7 %copy-start.4 = (s32[2]{0:T(128)S(1)}, s32[2]{0:T(128)}, u32[]{:S(2)}) copy-start(s32[2]{0:T(128)} %buckets.1) | copy-start | bytes 28

commit v2 on v1

--- a/solution.py
+++ b/solution.py
@@ -58,6 +58,7 @@
         ("prompts", prompts_h, prompts), ("frozen", frozen_h, frozen),
     )):
         loads[name] = pltpu.make_async_copy(src, dst, load_sem.at[n])
+    for name in ("og", "up", "acts", "down"):
         loads[name].start()
 
     x_peer = [lax.rem(x + d, F) for d in range(F)]
@@ -112,6 +113,8 @@
 
     loads["og"].wait()
     loads["up"].wait()
+    loads["prompts"].start()
+    loads["frozen"].start()
     slot = T // lengths.shape[0]
     position = lax.broadcasted_iota(jnp.int32, (slot, C), 0)
     for i in range(lengths.shape[0]):
@@ -133,8 +136,8 @@
     loads["frozen"].wait()
     tile_c = min(256, C)
 
-    def frozen_part(owner, put):
-        @pl.loop(0, C // tile_c)
+    def frozen_part(owner, put, first=0, last=C // tile_c):
+        @pl.loop(first, last)
         def _(t):
             cols = pl.ds(pl.multiple_of(t * tile_c, tile_c), tile_c)
             src = pl.ds(pl.multiple_of(owner * C + t * tile_c, tile_c), tile_c)
@@ -147,6 +150,8 @@
         frozen_part(x_peer[d], put_other)
 
     up_half = proj_sum(0, up_part)
+    for d in range(1, F):
+        send(gk.at[x], gk.at[x], x_send_sem.at[2, d], x_recv_sem.at[2, d], x_id(d))
     up_half_t = up_half.T.astype(BF16)
     up_half = up_half.astype(BF16)
     down_half_t = None
@@ -169,9 +174,6 @@
                     part = jnp.zeros((plan.rank, U), F32)
                 gbuf[k, s, i] = ADAPTER_SCALE * part
         send(*core_copy(k))
-
-    for d in range(1, F):
-        send(gk.at[x], gk.at[x], x_send_sem.at[2, d], x_recv_sem.at[2, d], x_id(d))
     for d in range(1, F):
         send(kp_send.at[d], kp_recv.at[d], x_send_sem.at[3, d], x_recv_sem.at[3, d], x_id(d))
 
@@ -195,10 +197,10 @@
     def put_own(cols, value):
         kp_own[:, cols] = value
 
-    frozen_part(x, put_own)
     pd[...] = jnp.dot(prompts[...], a_half[...], preferred_element_type=F32)
 
     part_rows = plan.rank // O
+    tiles_c = C // tile_c
     for k in range(K):
         value = quarter[k]
         for d in range(1, I):
@@ -209,6 +211,9 @@
             z_send[k, o] = value[o * part_rows:(o + 1) * part_rows].astype(BF16)
         for d in range(1, O):
             send(*z_copy(k, d))
+        first, last = k * tiles_c // K, (k + 1) * tiles_c // K
+        if first < last:
+            frozen_part(x, put_own, first, last)
 
     base = I + O
 
@@ -274,14 +279,16 @@
             )
         ig[:, span] = value.astype(BF16)
 
-    pl.loop(0, W // tile)(ig_tile)
-    ig_store = pltpu.make_async_copy(ig, ig_h, store_sem.at[0])
-    ig_store.start()
-
-    for k in range(K):
+    tiles = W // tile
+    for k in range(K):
+        first, last = k * tiles // K, (k + 1) * tiles // K
+        if first < last:
+            pl.loop(first, last)(ig_tile)
         for d in range(1, I):
             arrive(*ag_y(k, d, y_from[d]))
         send(*ag_core(k, core))
+    ig_store = pltpu.make_async_copy(ig, ig_h, store_sem.at[0])
+    ig_store.start()
     total = sq_sum(1, yi, I, y_id, lambda d: y_from[d])
     sq_send(2, total, core, S, lambda d: core_id)
     total = sq_sum(2, core, S, lambda d: core_id, lambda d: 1 - core)
@@ -334,6 +341,18 @@
     nd_store.wait()
     nu_store.wait()
     keys_store.wait()
+
+
+def move_kernel(pieces, *refs):
+    sem = refs[-1]
+    copies = []
+    for n, (which, row, count) in enumerate(pieces):
+        src, dst = refs[which], refs[4 + which]
+        span = pl.ds(row, count)
+        copies.append(pltpu.make_async_copy(src.at[span, :], dst.at[span, :], sem.at[n]))
+        copies[-1].start()
+    for copy in copies:
+        copy.wait()
 
 
 def per_device(mesh, acts, output_gradient, lengths, buckets, frozen, down, up, prompts):
@@ -364,7 +383,7 @@
         dma((6,)), dma((4,)), dma((4, F)), dma((4, F)), dma((K, hops)), dma((K, hops)),
         dma((4, max(O, I, S, F))), dma((4, max(O, I, S, F))),
     ]
-    return pl.pallas_call(
+    results = pl.pallas_call(
         functools.partial(kernel, plan),
         out_shape=(
             jax.ShapeDtypeStruct((T, W), BF16),
@@ -376,13 +395,25 @@
         out_specs=(hbm,) * 4,
         scratch_shapes=scratch,
         compiler_params=pltpu.CompilerParams(
-            collective_id=0, has_side_effects=True, vmem_limit_bytes=48 * 1024 * 1024
+            collective_id=0, has_side_effects=True, vmem_limit_bytes=60 * 1024 * 1024
         ),
         cost_estimate=pl.CostEstimate(
             flops=2 * T * W * (2 * N + 4 * R), bytes_accessed=2 * (3 * T * W + W * N), transcendentals=0
         ),
         name="adapter_step",
     )(lengths, buckets, acts, output_gradient, frozen, down, up, prompts)
+    pieces = [(0, n * T // 4, T // 4) for n in range(4)] + [
+        (1, n * W // 2, W // 2) for n in range(2)
+    ] + [(2, 0, R), (3, 0, T)]
+    return pl.pallas_call(
+        functools.partial(move_kernel, pieces),
+        out_shape=[jax.ShapeDtypeStruct(r.shape, r.dtype) for r in results],
+        in_specs=[hbm] * 4,
+        out_specs=[hbm] * 4,
+        scratch_shapes=[dma((len(pieces),))],
+        compiler_params=pltpu.CompilerParams(vmem_limit_bytes=60 * 1024 * 1024),
+        name="move_results",
+    )(*results)
 
 
 def solution(mesh):

time: 55.8 us -> 190 us (3.41)
  Pallas kernels: 44.3 us -> 189 us
  local copies, waits for them, and re-layouts: 10.6 us -> 0 us
    pallas_call x0 -> x1, Pallas kernels: none -> 144 us  [per_device(): pl.pallas_call(functools.partial(move_kernel, pieces), out_shape=[jax.Sha...]
    unnamed x14 -> x0, local copies, waits for them, and re-layouts: 10.6 us -> none
where the time goes in v2:
time: 190 us
  Pallas kernels  189 us (99%)
    pallas_call x1, Pallas kernels, per_device(): pl.pallas_call(functools.partial(move_kernel, pieces), out_shape=[jax.Sha...  144 us
    pallas_call x1, Pallas kernels, per_device(): pl.pallas_call(functools.partial(kernel, plan), out_shape=(jax.ShapeDtype...  45.2 us

profile of v2, /device:TPU:0, one launch (start us, length us, event | category | flops | bytes accessed | tf_op | source)
XLA Modules:
  0.0 190.0 jit_solution(13487027913927682130)
XLA Ops:
  0.6 45.2 %adapter_step.1 = (bf16[512,2560]{1,0:T(8,128)(2,1)}, f32[2560,128]{1,0:T(8,128)}, f32[128,512]{1,0:T(8,128)}, bf16[512,512]{1,0:T(8,128)(2,1)}) custom-call(s32[2]{0:T(128)} %lengths.1, s32[2]{0:T(128)} %buckets.1, bf16[512,2560]{1,0:T(8,128)(2,1)} %acts_h.1, bf16[512,512]{1,0:T(8,128)(2,1)} %og_h.1, bf16[2560,1024]{1,0:T(8,128)(2,1)} %frozen_h.1, ...), custom_call_target="tpu_custom_call" | custom-call | flops 6710886400 | bytes 13107200 | tf_op jit(solution)/shard_map/adapter_step/pallas_call | solution.py:386
  45.8 144.1 %move_results.1 = (bf16[512,2560]{1,0:T(8,128)(2,1)}, f32[2560,128]{1,0:T(8,128)}, f32[128,512]{1,0:T(8,128)}, bf16[512,512]{1,0:T(8,128)(2,1)}) custom-call(bf16[512,2560]{1,0:T(8,128)(2,1)} %get-tuple-element.8.refs_0_, f32[2560,128]{1,0:T(8,128)} %get-tuple-element.9.refs_1_, f32[128,512]{1,0:T(8,128)} %get-tuple-element.10.refs_2_, ...), custom_call_target="tpu_custom_call" | custom-call | tf_op jit(solution)/shard_map/move_results/pallas_call | solution.py:408

commit v3 on v2

--- a/solution.py
+++ b/solution.py
@@ -36,13 +36,12 @@
 def kernel(
     plan,
     lengths, buckets, acts_h, og_h, frozen_h, down_h, up_h, prompts_h,
-    ig_h, nd_h, nu_h, keys_h,
+    ig, nd, nu, keys,
     acts, og, frozen, down, up, prompts,
     a_half, gk, proj_send, proj_recv, pd, pg,
     kp_own, kp_send, kp_recv,
     gbuf, core_recv, y_send, y_recv, quarter, z_send, z_recv, ag, sq,
-    ig, nd, nu, keys,
-    load_sem, store_sem, x_send_sem, x_recv_sem, d_send_sem, d_recv_sem, q_send_sem, q_recv_sem,
+    load_sem, x_send_sem, x_recv_sem, d_send_sem, d_recv_sem, q_send_sem, q_recv_sem,
 ):
     F, S, I, O, K = plan.fsdp, plan.cores, plan.inner, plan.outer, plan.chunks
     U, W, C = plan.unit, plan.width, plan.channels
@@ -133,7 +132,7 @@
     proj_exchange(1, down_part)
 
     loads["prompts"].wait()
-    loads["frozen"].wait()
+    pd[...] = jnp.dot(prompts[...], a_half[...], preferred_element_type=F32)
     tile_c = min(256, C)
 
     def frozen_part(owner, put, first=0, last=C // tile_c):
@@ -142,12 +141,6 @@
             cols = pl.ds(pl.multiple_of(t * tile_c, tile_c), tile_c)
             src = pl.ds(pl.multiple_of(owner * C + t * tile_c, tile_c), tile_c)
             put(cols, jnp.dot(prompts[...], frozen[:, src], preferred_element_type=F32))
-
-    for d in range(1, F):
-        def put_other(cols, value, d=d):
-            kp_send[d, :, cols] = value.astype(BF16)
-
-        frozen_part(x_peer[d], put_other)
 
     up_half = proj_sum(0, up_part)
     for d in range(1, F):
@@ -174,9 +167,6 @@
                     part = jnp.zeros((plan.rank, U), F32)
                 gbuf[k, s, i] = ADAPTER_SCALE * part
         send(*core_copy(k))
-    for d in range(1, F):
-        send(kp_send.at[d], kp_recv.at[d], x_send_sem.at[3, d], x_recv_sem.at[3, d], x_id(d))
-
     def y_copy(k, d):
         return (y_send.at[k, d], y_recv.at[k, d], d_send_sem.at[k, d], d_recv_sem.at[k, d], y_id(d))
 
@@ -197,11 +187,21 @@
     def put_own(cols, value):
         kp_own[:, cols] = value
 
-    pd[...] = jnp.dot(prompts[...], a_half[...], preferred_element_type=F32)
-
+    loads["frozen"].wait()
     part_rows = plan.rank // O
     tiles_c = C // tile_c
-    for k in range(K):
+
+    def share(n, step):
+        return step * n // K, (step + 1) * n // K
+
+    for k in range(K):
+        first, last = share(tiles_c, K - 1 - k)
+        for d in range(1, F):
+            def put_other(cols, value, d=d):
+                kp_send[d, :, cols] = value.astype(BF16)
+
+            if first < last:
+                frozen_part(x_peer[d], put_other, first, last)
         value = quarter[k]
         for d in range(1, I):
             arrive(*y_copy(k, d))
@@ -211,9 +211,8 @@
             z_send[k, o] = value[o * part_rows:(o + 1) * part_rows].astype(BF16)
         for d in range(1, O):
             send(*z_copy(k, d))
-        first, last = k * tiles_c // K, (k + 1) * tiles_c // K
-        if first < last:
-            frozen_part(x, put_own, first, last)
+    for d in range(1, F):
+        send(kp_send.at[d], kp_recv.at[d], x_send_sem.at[3, d], x_recv_sem.at[3, d], x_id(d))
 
     base = I + O
 
@@ -231,6 +230,9 @@
 
     squares = jnp.zeros((part_rows, U), F32)
     for k in range(K):
+        first, last = share(tiles_c, K - 1 - k)
+        if first < last:
+            frozen_part(x, put_own, first, last)
         value = quarter[k, pl.ds(pl.multiple_of(zi * part_rows, part_rows), part_rows), :]
         for d in range(1, O):
             arrive(*z_copy(k, d))
@@ -281,14 +283,12 @@
 
     tiles = W // tile
     for k in range(K):
-        first, last = k * tiles // K, (k + 1) * tiles // K
+        first, last = share(tiles, k)
         if first < last:
             pl.loop(first, last)(ig_tile)
         for d in range(1, I):
             arrive(*ag_y(k, d, y_from[d]))
         send(*ag_core(k, core))
-    ig_store = pltpu.make_async_copy(ig, ig_h, store_sem.at[0])
-    ig_store.start()
     total = sq_sum(1, yi, I, y_id, lambda d: y_from[d])
     sq_send(2, total, core, S, lambda d: core_id)
     total = sq_sum(2, core, S, lambda d: core_id, lambda d: 1 - core)
@@ -320,10 +320,6 @@
         else:
             span = slice((n - plan.down_units) * U, (n - plan.down_units + 1) * U)
             nu[:, span] = up[:, span] - factor * unit_of(n).astype(F32)
-    nd_store = pltpu.make_async_copy(nd, nd_h, store_sem.at[1])
-    nd_store.start()
-    nu_store = pltpu.make_async_copy(nu, nu_h, store_sem.at[2])
-    nu_store.start()
 
     for d in range(1, F):
         arrive(kp_send.at[d], kp_recv.at[d], x_send_sem.at[3, d], x_recv_sem.at[3, d], x_id(d))
@@ -332,15 +328,9 @@
     keys[...] = (
         kp_own[...] + jnp.dot(low_half, nu[...].astype(BF16), preferred_element_type=F32)
     ).astype(BF16)
-    keys_store = pltpu.make_async_copy(keys, keys_h, store_sem.at[3])
-    keys_store.start()
 
     for copy in sent:
         copy.wait_send()
-    ig_store.wait()
-    nd_store.wait()
-    nu_store.wait()
-    keys_store.wait()
 
 
 def move_kernel(pieces, *refs):
@@ -364,6 +354,7 @@
     N = C * F
     smem = pl.BlockSpec(memory_space=pltpu.SMEM)
     hbm = pl.BlockSpec(memory_space=pl.ANY)
+    vmem = pl.BlockSpec(memory_space=pltpu.VMEM)
     dma = pltpu.SemaphoreType.DMA
     hops = I + O + O + I + 1
     scratch = [
@@ -379,39 +370,37 @@
         pltpu.VMEM((K, O, R // O, U), BF16), pltpu.VMEM((K, O, R // O, U), BF16),
         pltpu.VMEM((K, S, I, O, R // O, U), BF16),
         pltpu.VMEM((4, max(O, I, S, F), 8, 128), F32),
-        pltpu.VMEM((T, W), BF16), pltpu.VMEM((W, R), F32), pltpu.VMEM((R, C), F32), pltpu.VMEM((T, C), BF16),
-        dma((6,)), dma((4,)), dma((4, F)), dma((4, F)), dma((K, hops)), dma((K, hops)),
+        dma((6,)), dma((4, F)), dma((4, F)), dma((K, hops)), dma((K, hops)),
         dma((4, max(O, I, S, F))), dma((4, max(O, I, S, F))),
     ]
     results = pl.pallas_call(
         functools.partial(kernel, plan),
         out_shape=(
-            jax.ShapeDtypeStruct((T, W), BF16),
-            jax.ShapeDtypeStruct((W, R), F32),
-            jax.ShapeDtypeStruct((R, C), F32),
-            jax.ShapeDtypeStruct((T, C), BF16),
+            pltpu.VMEM((T, W), BF16), pltpu.VMEM((W, R), F32), pltpu.VMEM((R, C), F32), pltpu.VMEM((T, C), BF16),
         ),
         in_specs=[smem, smem] + [hbm] * 6,
-        out_specs=(hbm,) * 4,
+        out_specs=(vmem,) * 4,
         scratch_shapes=scratch,
         compiler_params=pltpu.CompilerParams(
-            collective_id=0, has_side_effects=True, vmem_limit_bytes=60 * 1024 * 1024
+            collective_id=0, has_side_effects=True, vmem_limit_bytes=48 * 1024 * 1024
         ),
         cost_estimate=pl.CostEstimate(
             flops=2 * T * W * (2 * N + 4 * R), bytes_accessed=2 * (3 * T * W + W * N), transcendentals=0
         ),
         name="adapter_step",
-    )(lengths, buckets, acts, output_gradient, frozen, down, up, prompts)
+    )(*(
+        pltpu.with_memory_space_constraint(a, pltpu.HBM)
+        for a in (lengths, buckets, acts, output_gradient, frozen, down, up, prompts)
+    ))
     pieces = [(0, n * T // 4, T // 4) for n in range(4)] + [
         (1, n * W // 2, W // 2) for n in range(2)
     ] + [(2, 0, R), (3, 0, T)]
     return pl.pallas_call(
         functools.partial(move_kernel, pieces),
-        out_shape=[jax.ShapeDtypeStruct(r.shape, r.dtype) for r in results],
-        in_specs=[hbm] * 4,
+        out_shape=[pltpu.HBM(r.shape, r.dtype) for r in results],
+        in_specs=[vmem] * 4,
         out_specs=[hbm] * 4,
         scratch_shapes=[dma((len(pieces),))],
-        compiler_params=pltpu.CompilerParams(vmem_limit_bytes=60 * 1024 * 1024),
         name="move_results",
     )(*results)
 

time: 190 us -> 53.8 us (0.28)
  Pallas kernels: 189 us -> 49 us
  local copies, waits for them, and re-layouts: 0 us -> 4.06 us
    pallas_call x2, Pallas kernels: 189 us -> 49 us  [the longest x1 44.4 us: per_device(): pl.pallas_call(functools.partial(kernel, plan), out_shape=(pltpu.VMEM((T,...]
    unnamed x0 -> x8, local copies, waits for them, and re-layouts: none -> 4.06 us
where the time goes in v3:
time: 53.8 us; the launch traced here: 53.7 us
  Pallas kernels  49 us (91%)
  local copies, waits for them, and re-layouts  4.06 us (8%)
  between operations  0.65 us (1%)
    pallas_call x1, Pallas kernels, per_device(): pl.pallas_call(functools.partial(kernel, plan), out_shape=(pltpu.VMEM((T,...  44.4 us
    pallas_call x1, Pallas kernels, per_device(): pl.pallas_call(functools.partial(move_kernel, pieces), out_shape=[pltpu.H...  4.54 us
    unnamed x8, local copies, waits for them, and re-layouts  4.06 us

profile of v3, /device:TPU:0, one launch (start us, length us, event | category | flops | bytes accessed | tf_op | source)
XLA Modules:
  0.0 53.7 jit_solution(17786129357911231660)
XLA Ops:
  0.6 44.4 %adapter_step.1 = (bf16[512,2560]{1,0:T(8,128)(2,1)S(1)}, f32[2560,128]{1,0:T(8,128)S(1)}, f32[128,512]{1,0:T(8,128)S(1)}, bf16[512,512]{1,0:T(8,128)(2,1)S(1)}) custom-call(s32[2]{0:T(128)} %lengths.1, s32[2]{0:T(128)} %buckets.1, bf16[512,2560]{1,0:T(8,128)(2,1)} %acts_h.1, bf16[512,512]{1,0:T(8,128)(2,1)} %og_h.1, bf16[2560,1024]{1,0:T(8,128)(2,1)} %frozen_h.1, ...), custom_call_target="tpu_custom_call" | custom-call | flops 6710886400 | bytes 13107200 | tf_op jit(solution)/shard_map/adapter_step/pallas_call | solution.py:376
  45.0 0.0 copy-start
  45.1 1.5 %copy-done = bf16[512,2560]{1,0:T(8,128)(2,1)} copy-done((bf16[512,2560]{1,0:T(8,128)(2,1)}, bf16[512,2560]{1,0:T(8,128)(2,1)S(1)}, u32[]{:S(2)}) %copy-start) | copy-done | bytes 2621464
  46.5 0.0 copy-start.1
  46.6 1.1 %copy-done.1 = f32[2560,128]{1,0:T(8,128)} copy-done((f32[2560,128]{1,0:T(8,128)}, f32[2560,128]{1,0:T(8,128)S(1)}, u32[]{:S(2)}) %copy-start.1) | copy-done | bytes 1310744
  47.6 0.0 copy-start.2
  47.6 0.8 %copy-done.2 = bf16[512,512]{1,0:T(8,128)(2,1)} copy-done((bf16[512,512]{1,0:T(8,128)(2,1)}, bf16[512,512]{1,0:T(8,128)(2,1)S(1)}, u32[]{:S(2)}) %copy-start.2) | copy-done | bytes 524312
  48.4 0.0 copy-start.3
  48.4 0.7 %copy-done.3 = f32[128,512]{1,0:T(8,128)} copy-done((f32[128,512]{1,0:T(8,128)}, f32[128,512]{1,0:T(8,128)S(1)}, u32[]{:S(2)}) %copy-start.3) | copy-done | bytes 262168
  49.1 4.5 %move_results.1 = (bf16[512,2560]{1,0:T(8,128)(2,1)}, f32[2560,128]{1,0:T(8,128)}, f32[128,512]{1,0:T(8,128)}, bf16[512,512]{1,0:T(8,128)(2,1)}) custom-call(bf16[512,2560]{1,0:T(8,128)(2,1)} %copy-done, f32[2560,128]{1,0:T(8,128)} %copy-done.1, f32[128,512]{1,0:T(8,128)} %copy-done.3, bf16[512,512]{1,0:T(8,128)(2,1)} %copy-done.2), custom_call_target="tpu_custom_call" | custom-call | tf_op jit(solution)/shard_map/move_results/pallas_call | solution.py:398
Async XLA Ops:
  45.0 1.5 %copy-start = (bf16[512,2560]{1,0:T(8,128)(2,1)}, bf16[512,2560]{1,0:T(8,128)(2,1)S(1)}, u32[]{:S(2)}) copy-start(bf16[512,2560]{1,0:T(8,128)(2,1)S(1)} %get-tuple-element.8.refs_0_) | copy-start | bytes 7864324
  46.5 1.1 %copy-start.1 = (f32[2560,128]{1,0:T(8,128)}, f32[2560,128]{1,0:T(8,128)S(1)}, u32[]{:S(2)}) copy-start(f32[2560,128]{1,0:T(8,128)S(1)} %get-tuple-element.9.refs_1_) | copy-start | bytes 3932164
  47.6 0.8 %copy-start.2 = (bf16[512,512]{1,0:T(8,128)(2,1)}, bf16[512,512]{1,0:T(8,128)(2,1)S(1)}, u32[]{:S(2)}) copy-start(bf16[512,512]{1,0:T(8,128)(2,1)S(1)} %get-tuple-element.11.refs_3_) | copy-start | bytes 1572868
  48.4 0.7 %copy-start.3 = (f32[128,512]{1,0:T(8,128)}, f32[128,512]{1,0:T(8,128)S(1)}, u32[]{:S(2)}) copy-start(f32[128,512]{1,0:T(8,128)S(1)} %get-tuple-element.10.refs_2_) | copy-start | bytes 786436

commit v4 on v3

--- a/solution.py
+++ b/solution.py
@@ -77,10 +77,16 @@
         return {"dp": z_peer[d] * I + yi}
 
     core_id = {"section": 1 - core}
-    others = (
-        [x_id(d) for d in range(1, F)] + [y_id(d) for d in range(1, I)]
-        + [z_id(d) for d in range(1, O)] + [core_id]
-    )
+
+    def dp_id(p):
+        return {"dp": p}
+
+    def group_id(p):
+        return {"fsdp": p // S, "section": p % S}
+
+    others = [dp_id(lax.rem(dp + d, O * I)) for d in range(1, O * I)] + [
+        group_id(lax.rem(x * S + core + d, F * S)) for d in range(1, F * S)
+    ]
     barrier = pltpu.get_barrier_semaphore()
     for other in others:
         pl.semaphore_signal(barrier, inc=1, device_id=other, device_id_type=MESH)
@@ -143,8 +149,6 @@
             put(cols, jnp.dot(prompts[...], frozen[:, src], preferred_element_type=F32))
 
     up_half = proj_sum(0, up_part)
-    for d in range(1, F):
-        send(gk.at[x], gk.at[x], x_send_sem.at[2, d], x_recv_sem.at[2, d], x_id(d))
     up_half_t = up_half.T.astype(BF16)
     up_half = up_half.astype(BF16)
     down_half_t = None
@@ -161,6 +165,8 @@
                 elif n < plan.units:
                     if down_half_t is None:
                         down_half_t = proj_sum(1, down_part).T.astype(BF16)
+                        for d in range(1, F):
+                            send(gk.at[x], gk.at[x], x_send_sem.at[4, d], x_recv_sem.at[4, d], x_id(d))
                     m = n - plan.down_units
                     part = jnp.dot(down_half_t, gk[x, :, m * U:(m + 1) * U], preferred_element_type=F32)
                 else:
@@ -211,8 +217,6 @@
             z_send[k, o] = value[o * part_rows:(o + 1) * part_rows].astype(BF16)
         for d in range(1, O):
             send(*z_copy(k, d))
-    for d in range(1, F):
-        send(kp_send.at[d], kp_recv.at[d], x_send_sem.at[3, d], x_recv_sem.at[3, d], x_id(d))
 
     base = I + O
 
@@ -244,32 +248,42 @@
         value = rounded.astype(F32)
         squares = squares + value * value
 
-    def sq_send(stage, value, own, count, to):
+    D, G = O * I, F * S
+    dp_peer = [lax.rem(dp + d, D) for d in range(D)]
+    group = x * S + core
+    group_peer = [lax.rem(group + d, G) for d in range(G)]
+
+    def sq_copy(stage, own, slot, d, to):
+        return (sq.at[stage, own], sq.at[stage, slot], q_send_sem.at[stage, d], q_recv_sem.at[stage, d], to)
+
+    def sq_send(stage, value, own, peers, to):
         sq[stage, own] = value
+        for d in range(1, len(peers)):
+            send(*sq_copy(stage, own, own, d, to(peers[d])))
+
+    def sq_sum(stage, own, peers, to):
+        count = len(peers)
         for d in range(1, count):
-            send(sq.at[stage, own], sq.at[stage, own], q_send_sem.at[stage, d], q_recv_sem.at[stage, d], to(d))
-
-    def sq_sum(stage, own, count, to, source):
-        for d in range(1, count):
-            arrive(sq.at[stage, own], sq.at[stage, source(d)], q_send_sem.at[stage, d], q_recv_sem.at[stage, d], to(d))
+            arrive(*sq_copy(stage, own, lax.rem(own + count - d, count), d, to(peers[d])))
         total = sq[stage, 0]
         for n in range(1, count):
             total = total + sq[stage, n]
         return total
 
     total = jnp.broadcast_to(jnp.sum(squares, keepdims=True), (8, 128))
-    sq_send(0, total, zi, O, z_id)
+    sq_send(0, total, dp, dp_peer, dp_id)
 
     for k in range(K):
         for d in range(1, O):
             arrive(*ag_z(k, d, z_from[d]))
         for d in range(1, I):
             send(*ag_y(k, d, yi))
-    total = sq_sum(0, zi, O, z_id, lambda d: z_from[d])
-    sq_send(1, total, yi, I, y_id)
+    sq_send(1, sq_sum(0, dp, dp_peer, dp_id), group, group_peer, group_id)
 
     for d in range(1, F):
-        arrive(gk.at[x], gk.at[x_from[d]], x_send_sem.at[2, d], x_recv_sem.at[2, d], x_id(d))
+        arrive(gk.at[x], gk.at[x_from[d]], x_send_sem.at[4, d], x_recv_sem.at[4, d], x_id(d))
+    for d in range(1, F):
+        send(kp_send.at[d], kp_recv.at[d], x_send_sem.at[3, d], x_recv_sem.at[3, d], x_id(d))
     tile = plan.tile
 
     def ig_tile(t):
@@ -289,10 +303,6 @@
         for d in range(1, I):
             arrive(*ag_y(k, d, y_from[d]))
         send(*ag_core(k, core))
-    total = sq_sum(1, yi, I, y_id, lambda d: y_from[d])
-    sq_send(2, total, core, S, lambda d: core_id)
-    total = sq_sum(2, core, S, lambda d: core_id, lambda d: 1 - core)
-    sq_send(3, total, x, F, x_id)
 
     def unit_of(n):
         k, s, i = n // (S * I), (n // I) % S, n % I
@@ -306,7 +316,7 @@
                 low = low + lax.dot_general(
                     prompts[:, n * U:(n + 1) * U], unit_of(n), NT, preferred_element_type=F32
                 )
-    total = sq_sum(3, x, F, x_id, lambda d: x_from[d])
+    total = sq_sum(1, group, group_peer, group_id)
     norm = jnp.sqrt(total + 1e-12)
     factor = (STEP_RATE * jnp.minimum(1.0, CLIP_NORM / norm))[0:1, 0:1]
 
@@ -369,9 +379,9 @@
         pltpu.VMEM((K, R, U), F32),
         pltpu.VMEM((K, O, R // O, U), BF16), pltpu.VMEM((K, O, R // O, U), BF16),
         pltpu.VMEM((K, S, I, O, R // O, U), BF16),
-        pltpu.VMEM((4, max(O, I, S, F), 8, 128), F32),
-        dma((6,)), dma((4, F)), dma((4, F)), dma((K, hops)), dma((K, hops)),
-        dma((4, max(O, I, S, F))), dma((4, max(O, I, S, F))),
+        pltpu.VMEM((2, max(O * I, F * S), 8, 128), F32),
+        dma((6,)), dma((5, F)), dma((5, F)), dma((K, hops)), dma((K, hops)),
+        dma((2, max(O * I, F * S))), dma((2, max(O * I, F * S))),
     ]
     results = pl.pallas_call(
         functools.partial(kernel, plan),
@@ -401,8 +411,9 @@
         in_specs=[vmem] * 4,
         out_specs=[hbm] * 4,
         scratch_shapes=[dma((len(pieces),))],
+        compiler_params=pltpu.CompilerParams(vmem_limit_bytes=16 * 1024 * 1024),
         name="move_results",
-    )(*results)
+    )(*(pltpu.with_memory_space_constraint(r, pltpu.VMEM) for r in results))
 
 
 def solution(mesh):

time: 53.8 us -> 48.1 us (0.89)
  local copies, waits for them, and re-layouts: 4.06 us -> 0 us
  Pallas kernels: 49 us -> 47.3 us
    unnamed x8 -> x0, local copies, waits for them, and re-layouts: 4.06 us -> none
    pallas_call x1, Pallas kernels: 4.54 us -> 2.25 us  [per_device(): pl.pallas_call(functools.partial(move_kernel, pieces), out_shape=[pltpu.H...]
    pallas_call x1, Pallas kernels: 44.4 us -> 45.1 us  [per_device(): pl.pallas_call(functools.partial(kernel, plan), out_shape=(pltpu.VMEM((T,...]
where the time goes in v4:
time: 48.1 us; the launch traced here: 47.9 us
  Pallas kernels  47.3 us (98%)
  between operations  0.64 us (1%)
    pallas_call x1, Pallas kernels, per_device(): pl.pallas_call(functools.partial(kernel, plan), out_shape=(pltpu.VMEM((T,...  45.1 us
    pallas_call x1, Pallas kernels, per_device(): pl.pallas_call(functools.partial(move_kernel, pieces), out_shape=[pltpu.H...  2.25 us

profile of v4, /device:TPU:0, one launch (start us, length us, event | category | flops | bytes accessed | tf_op | source)
XLA Modules:
  0.0 47.9 jit_solution(350667375770527655)
XLA Ops:
  0.6 45.1 %adapter_step.1 = (bf16[512,2560]{1,0:T(8,128)(2,1)S(1)}, f32[2560,128]{1,0:T(8,128)S(1)}, f32[128,512]{1,0:T(8,128)S(1)}, bf16[512,512]{1,0:T(8,128)(2,1)S(1)}) custom-call(s32[2]{0:T(128)} %lengths.1, s32[2]{0:T(128)} %buckets.1, bf16[512,2560]{1,0:T(8,128)(2,1)} %acts_h.1, bf16[512,512]{1,0:T(8,128)(2,1)} %og_h.1, bf16[2560,1024]{1,0:T(8,128)(2,1)} %frozen_h.1, ...), custom_call_target="tpu_custom_call" | custom-call | flops 6710886400 | bytes 13107200 | tf_op jit(solution)/shard_map/adapter_step/pallas_call | solution.py:386
  45.7 2.2 %move_results.1 = (bf16[512,2560]{1,0:T(8,128)(2,1)}, f32[2560,128]{1,0:T(8,128)}, f32[128,512]{1,0:T(8,128)}, bf16[512,512]{1,0:T(8,128)(2,1)}) custom-call(bf16[512,2560]{1,0:T(8,128)(2,1)S(1)} %get-tuple-element.8.refs_0_, f32[2560,128]{1,0:T(8,128)S(1)} %get-tuple-element.9.refs_1_, f32[128,512]{1,0:T(8,128)S(1)} %get-tuple-element.10.refs_2_, ...), custom_call_target="tpu_custom_call" | custom-call | tf_op jit(solution)/shard_map/move_results/pallas_call | solution.py:408

commit v5 on v4

--- a/solution.py
+++ b/solution.py
@@ -149,6 +149,8 @@
             put(cols, jnp.dot(prompts[...], frozen[:, src], preferred_element_type=F32))
 
     up_half = proj_sum(0, up_part)
+    for d in range(1, F):
+        send(gk.at[x], gk.at[x], x_send_sem.at[4, d], x_recv_sem.at[4, d], x_id(d))
     up_half_t = up_half.T.astype(BF16)
     up_half = up_half.astype(BF16)
     down_half_t = None
@@ -165,8 +167,6 @@
                 elif n < plan.units:
                     if down_half_t is None:
                         down_half_t = proj_sum(1, down_part).T.astype(BF16)
-                        for d in range(1, F):
-                            send(gk.at[x], gk.at[x], x_send_sem.at[4, d], x_recv_sem.at[4, d], x_id(d))
                     m = n - plan.down_units
                     part = jnp.dot(down_half_t, gk[x, :, m * U:(m + 1) * U], preferred_element_type=F32)
                 else:
@@ -217,6 +217,16 @@
             z_send[k, o] = value[o * part_rows:(o + 1) * part_rows].astype(BF16)
         for d in range(1, O):
             send(*z_copy(k, d))
+
+    def kp_copy(half, d):
+        span = pl.ds(half * (T // 2), T // 2)
+        n = (3, 5)[half]
+        return (
+            kp_send.at[d, span, :], kp_recv.at[d, span, :], x_send_sem.at[n, d], x_recv_sem.at[n, d], x_id(d)
+        )
+
+    for d in range(1, F):
+        send(*kp_copy(0, d))
 
     base = I + O
 
@@ -280,10 +290,15 @@
             send(*ag_y(k, d, yi))
     sq_send(1, sq_sum(0, dp, dp_peer, dp_id), group, group_peer, group_id)
 
+    for k in range(K):
+        for d in range(1, I):
+            arrive(*ag_y(k, d, y_from[d]))
+        send(*ag_core(k, core))
+
     for d in range(1, F):
         arrive(gk.at[x], gk.at[x_from[d]], x_send_sem.at[4, d], x_recv_sem.at[4, d], x_id(d))
     for d in range(1, F):
-        send(kp_send.at[d], kp_recv.at[d], x_send_sem.at[3, d], x_recv_sem.at[3, d], x_id(d))
+        send(*kp_copy(1, d))
     tile = plan.tile
 
     def ig_tile(t):
@@ -296,20 +311,16 @@
         ig[:, span] = value.astype(BF16)
 
     tiles = W // tile
+
+    def unit_of(n):
+        k, s, i = n // (S * I), (n // I) % S, n % I
+        return ag[k, s, i].reshape(plan.rank, U)
+
+    low = jnp.zeros((T, plan.rank), F32)
     for k in range(K):
         first, last = share(tiles, k)
         if first < last:
             pl.loop(first, last)(ig_tile)
-        for d in range(1, I):
-            arrive(*ag_y(k, d, y_from[d]))
-        send(*ag_core(k, core))
-
-    def unit_of(n):
-        k, s, i = n // (S * I), (n // I) % S, n % I
-        return ag[k, s, i].reshape(plan.rank, U)
-
-    low = jnp.zeros((T, plan.rank), F32)
-    for k in range(K):
         arrive(*ag_core(k, 1 - core))
         for n in range(k * S * I, (k + 1) * S * I):
             if n < plan.down_units:
@@ -332,7 +343,8 @@
             nu[:, span] = up[:, span] - factor * unit_of(n).astype(F32)
 
     for d in range(1, F):
-        arrive(kp_send.at[d], kp_recv.at[d], x_send_sem.at[3, d], x_recv_sem.at[3, d], x_id(d))
+        for half in range(2):
+            arrive(*kp_copy(half, d))
         kp_own[...] = kp_own[...] + kp_recv[d].astype(F32)
     low_half = (ADAPTER_SCALE * proj_sum(2, pg[...])).astype(BF16)
     keys[...] = (
@@ -380,7 +392,7 @@
         pltpu.VMEM((K, O, R // O, U), BF16), pltpu.VMEM((K, O, R // O, U), BF16),
         pltpu.VMEM((K, S, I, O, R // O, U), BF16),
         pltpu.VMEM((2, max(O * I, F * S), 8, 128), F32),
-        dma((6,)), dma((5, F)), dma((5, F)), dma((K, hops)), dma((K, hops)),
+        dma((6,)), dma((6, F)), dma((6, F)), dma((K, hops)), dma((K, hops)),
         dma((2, max(O * I, F * S))), dma((2, max(O * I, F * S))),
     ]
     results = pl.pallas_call(

time: 48.1 us -> 47.9 us (level)
  no operation moved by 1% of the time
where the time goes in v5:
time: 47.9 us; the launch traced here: 47.7 us
  Pallas kernels  47.1 us (98%)
  between operations  0.64 us (1%)
    pallas_call x1, Pallas kernels, per_device(): pl.pallas_call(functools.partial(kernel, plan), out_shape=(pltpu.VMEM((T,...  44.8 us
    pallas_call x1, Pallas kernels, per_device(): pl.pallas_call(functools.partial(move_kernel, pieces), out_shape=[pltpu.H...  2.25 us

profile of v5, /device:TPU:0, one launch (start us, length us, event | category | flops | bytes accessed | tf_op | source)
XLA Modules:
  0.0 47.7 jit_solution(15822644081180227940)
XLA Ops:
  0.6 44.8 %adapter_step.1 = (bf16[512,2560]{1,0:T(8,128)(2,1)S(1)}, f32[2560,128]{1,0:T(8,128)S(1)}, f32[128,512]{1,0:T(8,128)S(1)}, bf16[512,512]{1,0:T(8,128)(2,1)S(1)}) custom-call(s32[2]{0:T(128)} %lengths.1, s32[2]{0:T(128)} %buckets.1, bf16[512,2560]{1,0:T(8,128)(2,1)} %acts_h.1, bf16[512,512]{1,0:T(8,128)(2,1)} %og_h.1, bf16[2560,1024]{1,0:T(8,128)(2,1)} %frozen_h.1, ...), custom_call_target="tpu_custom_call" | custom-call | flops 6710886400 | bytes 13107200 | tf_op jit(solution)/shard_map/adapter_step/pallas_call | solution.py:398
  45.5 2.2 %move_results.1 = (bf16[512,2560]{1,0:T(8,128)(2,1)}, f32[2560,128]{1,0:T(8,128)}, f32[128,512]{1,0:T(8,128)}, bf16[512,512]{1,0:T(8,128)(2,1)}) custom-call(bf16[512,2560]{1,0:T(8,128)(2,1)S(1)} %get-tuple-element.8.refs_0_, f32[2560,128]{1,0:T(8,128)S(1)} %get-tuple-element.9.refs_1_, f32[128,512]{1,0:T(8,128)S(1)} %get-tuple-element.10.refs_2_, ...), custom_call_target="tpu_custom_call" | custom-call | tf_op jit(solution)/shard_map/move_results/pallas_call | solution.py:420
